TPU v7x, 32 devices: a whole 2x2x4 slice. The times are simulated.
32 devices in a mesh: fsdp: 2 (over x), ctx: 4 (over y, core), tp: 4 (over z).
Axes of the slice: x: 2, y: 2, z: 4, core: 2. Of those that a mesh axis runs over, the one named last changes fastest.
Arguments:
- tokens: bfloat16 [2, 2048, 2304], P('fsdp', 'ctx'), may hold values from -6 to 6
- q_weight: bfloat16 [2304, 2048], P(('fsdp', 'ctx'), 'tp'), as said below
- key_weight: bfloat16 [2304, 1024], P(('fsdp', 'ctx'), 'tp'), may hold values from -0.125 to 0.125
- value_weight: bfloat16 [2304, 1024], P(('fsdp', 'ctx'), 'tp'), may hold values from -0.125 to 0.125
- out_weight: bfloat16 [2048, 2304], P('tp', ('fsdp', 'ctx')), may hold values from -0.125 to 0.125
- gate_weight: bfloat16 [2304, 9216], P(('fsdp', 'ctx'), 'tp'), may hold values from -0.125 to 0.125
- up_weight: bfloat16 [2304, 9216], P(('fsdp', 'ctx'), 'tp'), may hold values from -0.125 to 0.125
- down_weight: bfloat16 [9216, 2304], P('tp', ('fsdp', 'ctx')), may hold values from -0.0625 to 0.0625
- gain_attn_in: bfloat16 [2304], P(('fsdp', 'ctx')), may hold values from 0.099609375 to 1.8984375
- gain_attn_out: bfloat16 [2304], P(('fsdp', 'ctx')), may hold values from 0.099609375 to 1.8984375
- gain_mlp_in: bfloat16 [2304], P(('fsdp', 'ctx')), may hold values from 0.099609375 to 1.8984375
- gain_mlp_out: bfloat16 [2304], P(('fsdp', 'ctx')), may hold values from 0.099609375 to 1.8984375
- segment_ids: int32 [2, 2048], P('fsdp'), may hold values from 0 to 4, as said below
- block_order: int32 [2, 8], P('fsdp'), may hold values from 0 to 7, as said below
- cotangent: bfloat16 [2, 2048, 2304], P('fsdp', 'ctx'), may hold values from -6 to 6
Outputs:
- layer_out: bfloat16 [2, 2048, 2304], P('fsdp', 'ctx')
- grad_tokens: float32 [2, 2048, 2304], P('fsdp', 'ctx')
- grad_q_weight: float32 [2304, 2048], P(('fsdp', 'ctx'), 'tp')
- grad_key_weight: float32 [2304, 1024], P(('fsdp', 'ctx'), 'tp')
- grad_value_weight: float32 [2304, 1024], P(('fsdp', 'ctx'), 'tp')
- grad_out_weight: float32 [2048, 2304], P('tp', ('fsdp', 'ctx'))
- grad_gate_weight: float32 [2304, 9216], P(('fsdp', 'ctx'), 'tp')
- grad_up_weight: float32 [2304, 9216], P(('fsdp', 'ctx'), 'tp')
- grad_down_weight: float32 [9216, 2304], P('tp', ('fsdp', 'ctx'))
- grad_gain_attn_in: float32 [2304], P(('fsdp', 'ctx'))
- grad_gain_attn_out: float32 [2304], P(('fsdp', 'ctx'))
- grad_gain_mlp_in: float32 [2304], P(('fsdp', 'ctx'))
- grad_gain_mlp_out: float32 [2304], P(('fsdp', 'ctx'))
Inputs may be any that keep to these rules, and one draw needn't show every extreme that they name: `segment_ids`: along each sequence the ids never fall; every one of the 5 documents is present; document 0 covers at least the first 1024 positions. `block_order`: each row is a permutation of the 8 blocks; stored blocks 2j and 2j + 1 hold true blocks b and 7 - b for some b. `q_weight`: every entry is at most 24 / sqrt(2304) in magnitude.
All inputs are finite; a program needn't handle non-finite values.
Results may differ from a plain program's by a relative error of at most 0.023.
The roundings to bfloat16 on the way count: a program that leaves them out, or rounds other values in their place, can miss the bound.
Values may be sent and summed in bfloat16 or wider, within the bound.
No kernel may reach another device: no remote copies, remote signals or barrier semaphores. Data moves between devices by JAX's collectives and lax.ppermute only.
A program may use at most 256 MiB of HBM per device.

v0:
```python
import jax
import jax.numpy as jnp
from jax import lax
from jax.sharding import PartitionSpec as P

HEAD_DIM = 256
BLOCK = 256
EPS = 1e-06
CAP = 50.0
THETA = 10000.0


def normalize(values, gain):
    return (
        values
        * lax.rsqrt(jnp.mean(values * values, axis=-1, keepdims=True) + EPS)
        * gain.astype(jnp.float32)
    )


def normalize_back(values, gain, upstream):
    inverse = lax.rsqrt(jnp.mean(values * values, axis=-1, keepdims=True) + EPS)
    scaled = upstream * gain.astype(jnp.float32)
    d_values = inverse * scaled - values * inverse * inverse * inverse * jnp.mean(
        scaled * values, axis=-1, keepdims=True
    )
    d_gain = jnp.sum(upstream * values * inverse, axis=0)
    return (d_values, d_gain)


def angles_for(positions, width):
    half = width // 2
    freqs = THETA ** (-jnp.arange(half, dtype=jnp.float32) * 2.0 / width)
    angles = positions.astype(jnp.float32)[:, None] * freqs[None, :]
    return (jnp.cos(angles)[:, None, :], jnp.sin(angles)[:, None, :], half)


def rotate(values, positions):
    cosine, sine, half = angles_for(positions, values.shape[-1])
    first = values[..., :half]
    second = values[..., half:]
    return jnp.concatenate(
        [first * cosine - second * sine, second * cosine + first * sine], axis=-1
    )


def rotate_back(grads, positions):
    cosine, sine, half = angles_for(positions, grads.shape[-1])
    first = grads[..., :half]
    second = grads[..., half:]
    return jnp.concatenate(
        [first * cosine + second * sine, second * cosine - first * sine], axis=-1
    )


def outer(left, right):
    return lax.dot_general(
        left, right, (((0,), (0,)), ((), ())), preferred_element_type=jnp.float32
    )


def times_transposed(left, right):
    return lax.dot_general(
        left, right, (((1,), (1,)), ((), ())), preferred_element_type=jnp.float32
    )


def masked_scores(query_block, pos_block, seg_block, keys_all, key_pos, key_seg):
    scores = jnp.einsum("rd,kd->rk", query_block, keys_all, preferred_element_type=jnp.float32)
    bent = jnp.tanh(scores / CAP)
    allowed = (seg_block[:, None] == key_seg[None, :]) & (
        (pos_block // BLOCK)[:, None] >= (key_pos // BLOCK)[None, :]
    )
    return (jnp.where(allowed, CAP * bent, -1e30), bent)


def per_device(
    tokens,
    q_weight,
    key_weight,
    value_weight,
    out_weight,
    gate_weight,
    up_weight,
    down_weight,
    gain_attn_in,
    gain_attn_out,
    gain_mlp_in,
    gain_mlp_out,
    segment_ids,
    block_order,
    cotangent,
):
    inputs = tokens[0].astype(jnp.float32)
    tok_count = inputs.shape[0]
    q_full, key_full, value_full, out_full, gain_one, gain_two = (
        lax.all_gather(q_weight, ("fsdp", "ctx"), axis=0, tiled=True),
        lax.all_gather(key_weight, ("fsdp", "ctx"), axis=0, tiled=True),
        lax.all_gather(value_weight, ("fsdp", "ctx"), axis=0, tiled=True),
        lax.all_gather(out_weight, ("fsdp", "ctx"), axis=1, tiled=True),
        lax.all_gather(gain_attn_in, ("fsdp", "ctx"), axis=0, tiled=True),
        lax.all_gather(gain_attn_out, ("fsdp", "ctx"), axis=0, tiled=True),
    )
    order = block_order[0]
    within = jnp.arange(BLOCK, dtype=jnp.int32)
    key_pos = (order[:, None] * BLOCK + within[None, :]).reshape(-1)
    key_seg = segment_ids[0].reshape(-1, BLOCK)[order].reshape(-1)
    start = lax.axis_index("ctx") * tok_count
    query_pos = lax.dynamic_slice_in_dim(key_pos, start, tok_count)
    query_seg = lax.dynamic_slice_in_dim(key_seg, start, tok_count)
    normed_attn = normalize(inputs, gain_one).astype(jnp.bfloat16)
    q_lin = jnp.dot(normed_attn, q_full, preferred_element_type=jnp.float32)
    heads_local = q_lin.shape[1] // HEAD_DIM
    scale = HEAD_DIM ** (-0.5)
    queries = (rotate(q_lin.reshape(tok_count, heads_local, HEAD_DIM), query_pos) * scale).astype(
        jnp.bfloat16
    )
    key_lin = jnp.dot(normed_attn, key_full, preferred_element_type=jnp.float32)
    keys_own = rotate(key_lin[:, None, :], query_pos)[:, 0, :].astype(jnp.bfloat16)
    values_own = jnp.dot(normed_attn, value_full, preferred_element_type=jnp.float32).astype(
        jnp.bfloat16
    )
    keys_all, values_all = (
        lax.all_gather(keys_own, "ctx", axis=0, tiled=True),
        lax.all_gather(values_own, "ctx", axis=0, tiled=True),
    )
    rows = min(512, tok_count)
    blocks = tok_count // rows
    query_items = queries.transpose(1, 0, 2)
    pos_items = jnp.tile(query_pos.reshape(blocks, rows), (heads_local, 1))
    seg_items = jnp.tile(query_seg.reshape(blocks, rows), (heads_local, 1))

    def forward_item(item):
        query_block, pos_block, seg_block = item
        masked, bent = masked_scores(query_block, pos_block, seg_block, keys_all, key_pos, key_seg)
        highest = jnp.max(masked, axis=-1, keepdims=True)
        expo = jnp.exp(masked - highest)
        total = jnp.sum(expo, axis=-1, keepdims=True)
        weights = (expo / total).astype(jnp.bfloat16)
        output = jnp.einsum("rk,kd->rd", weights, values_all, preferred_element_type=jnp.float32)
        return (output, (highest + jnp.log(total))[:, 0])

    outputs, logsums = lax.map(forward_item, (query_items, pos_items, seg_items))
    attended = (
        outputs.transpose(1, 0, 2).reshape(tok_count, heads_local * HEAD_DIM).astype(jnp.bfloat16)
    )
    branch_attn = lax.psum(jnp.dot(attended, out_full, preferred_element_type=jnp.float32), "tp")
    resid = inputs + normalize(branch_attn, gain_two)
    gate_full, up_full, down_full, gain_three, gain_four = (
        lax.all_gather(gate_weight, ("fsdp", "ctx"), axis=0, tiled=True),
        lax.all_gather(up_weight, ("fsdp", "ctx"), axis=0, tiled=True),
        lax.all_gather(down_weight, ("fsdp", "ctx"), axis=1, tiled=True),
        lax.all_gather(gain_mlp_in, ("fsdp", "ctx"), axis=0, tiled=True),
        lax.all_gather(gain_mlp_out, ("fsdp", "ctx"), axis=0, tiled=True),
    )
    normed_mlp = normalize(resid, gain_three).astype(jnp.bfloat16)
    gate_lin = jnp.dot(normed_mlp, gate_full, preferred_element_type=jnp.float32)
    up_lin = jnp.dot(normed_mlp, up_full, preferred_element_type=jnp.float32)
    activ = (jax.nn.gelu(gate_lin, approximate=True) * up_lin).astype(jnp.bfloat16)
    branch_mlp = lax.psum(jnp.dot(activ, down_full, preferred_element_type=jnp.float32), "tp")
    layer_out = resid + normalize(branch_mlp, gain_four)
    upstream = cotangent[0].astype(jnp.float32)
    d_branch_mlp, grad_gain_four = normalize_back(branch_mlp, gain_four, upstream)
    d_mlp_low = d_branch_mlp.astype(jnp.bfloat16)
    grad_down = outer(activ, d_mlp_low)
    d_activ = times_transposed(d_mlp_low, down_full)
    unused_value, gelu_pullback = jax.vjp(
        lambda gate_in, up_in: jax.nn.gelu(gate_in, approximate=True) * up_in, gate_lin, up_lin
    )
    d_gate, d_up = gelu_pullback(d_activ)
    d_gate_low = d_gate.astype(jnp.bfloat16)
    d_up_low = d_up.astype(jnp.bfloat16)
    grad_gate = outer(normed_mlp, d_gate_low)
    grad_up = outer(normed_mlp, d_up_low)
    d_normed_mlp = lax.psum(
        times_transposed(d_gate_low, gate_full) + times_transposed(d_up_low, up_full), "tp"
    )
    d_resid_mlp, grad_gain_three = normalize_back(resid, gain_three, d_normed_mlp)
    d_resid = upstream + d_resid_mlp
    d_branch_attn, grad_gain_two = normalize_back(branch_attn, gain_two, d_resid)
    d_attn_low = d_branch_attn.astype(jnp.bfloat16)
    grad_out = outer(attended, d_attn_low)
    d_attended = times_transposed(d_attn_low, out_full).astype(jnp.bfloat16)
    d_items = d_attended.reshape(tok_count, heads_local, HEAD_DIM).transpose(1, 0, 2)

    def backward_item(sums, item):
        query_block, pos_block, seg_block, d_out, logsum = item
        masked, bent = masked_scores(query_block, pos_block, seg_block, keys_all, key_pos, key_seg)
        probs = jnp.exp(masked - logsum[:, None])
        weights = probs.astype(jnp.bfloat16)
        d_weights = jnp.einsum("rd,kd->rk", d_out, values_all, preferred_element_type=jnp.float32)
        d_values_sum = sums[1] + jnp.einsum(
            "rk,rd->kd", weights, d_out, preferred_element_type=jnp.float32
        )
        inner = jnp.sum(probs * d_weights, axis=-1, keepdims=True)
        d_scores = (probs * (d_weights - inner) * (1.0 - bent * bent)).astype(jnp.bfloat16)
        d_query = jnp.einsum("rk,kd->rd", d_scores, keys_all, preferred_element_type=jnp.float32)
        d_keys_sum = sums[0] + jnp.einsum(
            "rk,rd->kd", d_scores, query_block, preferred_element_type=jnp.float32
        )
        return ((d_keys_sum, d_values_sum), d_query)

    zeros_kv = jnp.zeros(keys_all.shape, jnp.float32)
    (d_keys_every, d_values_every), d_query_items = lax.scan(
        backward_item, (zeros_kv, zeros_kv), (query_items, pos_items, seg_items, d_items, logsums)
    )
    d_keys_rot, d_values_mine = (
        lax.psum_scatter(d_keys_every, "ctx", scatter_dimension=0, tiled=True),
        lax.psum_scatter(d_values_every, "ctx", scatter_dimension=0, tiled=True),
    )
    d_key_lin = rotate_back(d_keys_rot[:, None, :], query_pos)[:, 0, :].astype(jnp.bfloat16)
    d_value_lin = d_values_mine.astype(jnp.bfloat16)
    d_queries = d_query_items.transpose(1, 0, 2)
    d_q_lin = (
        rotate_back(d_queries * scale, query_pos)
        .reshape(tok_count, heads_local * HEAD_DIM)
        .astype(jnp.bfloat16)
    )
    grad_query = outer(normed_attn, d_q_lin)
    grad_key = outer(normed_attn, d_key_lin)
    grad_value = outer(normed_attn, d_value_lin)
    d_normed_attn = lax.psum(
        (
            times_transposed(d_q_lin, q_full)
            + times_transposed(d_key_lin, key_full)
            + times_transposed(d_value_lin, value_full)
        ).astype(jnp.bfloat16),
        "tp",
    ).astype(jnp.float32)
    d_tokens_attn, grad_gain_one = normalize_back(inputs, gain_one, d_normed_attn)
    grad_tokens = d_resid + d_tokens_attn
    every_grad = (
        lax.psum_scatter(
            grad_query.astype(jnp.bfloat16), ("fsdp", "ctx"), scatter_dimension=0, tiled=True
        ).astype(jnp.float32),
        lax.psum_scatter(
            grad_key.astype(jnp.bfloat16), ("fsdp", "ctx"), scatter_dimension=0, tiled=True
        ).astype(jnp.float32),
        lax.psum_scatter(
            grad_value.astype(jnp.bfloat16), ("fsdp", "ctx"), scatter_dimension=0, tiled=True
        ).astype(jnp.float32),
        lax.psum_scatter(
            grad_out.astype(jnp.bfloat16), ("fsdp", "ctx"), scatter_dimension=1, tiled=True
        ).astype(jnp.float32),
        lax.psum_scatter(
            grad_gain_one.astype(jnp.bfloat16), ("fsdp", "ctx"), scatter_dimension=0, tiled=True
        ).astype(jnp.float32),
        lax.psum_scatter(
            grad_gain_two.astype(jnp.bfloat16), ("fsdp", "ctx"), scatter_dimension=0, tiled=True
        ).astype(jnp.float32),
        lax.psum_scatter(
            grad_gate.astype(jnp.bfloat16), ("fsdp", "ctx"), scatter_dimension=0, tiled=True
        ).astype(jnp.float32),
        lax.psum_scatter(
            grad_up.astype(jnp.bfloat16), ("fsdp", "ctx"), scatter_dimension=0, tiled=True
        ).astype(jnp.float32),
        lax.psum_scatter(
            grad_down.astype(jnp.bfloat16), ("fsdp", "ctx"), scatter_dimension=1, tiled=True
        ).astype(jnp.float32),
        lax.psum_scatter(
            grad_gain_three.astype(jnp.bfloat16), ("fsdp", "ctx"), scatter_dimension=0, tiled=True
        ).astype(jnp.float32),
        lax.psum_scatter(
            grad_gain_four.astype(jnp.bfloat16), ("fsdp", "ctx"), scatter_dimension=0, tiled=True
        ).astype(jnp.float32),
    )
    attn_results = every_grad[:6]
    mlp_results = every_grad[6:]
    return (
        layer_out.astype(jnp.bfloat16)[None],
        grad_tokens[None],
        attn_results[0],
        attn_results[1],
        attn_results[2],
        attn_results[3],
        mlp_results[0],
        mlp_results[1],
        mlp_results[2],
        attn_results[4],
        attn_results[5],
        mlp_results[3],
        mlp_results[4],
    )


def solution(mesh):
    return jax.shard_map(
        per_device,
        mesh=mesh,
        in_specs=(
            P("fsdp", "ctx", None),
            P(("fsdp", "ctx"), "tp"),
            P(("fsdp", "ctx"), "tp"),
            P(("fsdp", "ctx"), "tp"),
            P("tp", ("fsdp", "ctx")),
            P(("fsdp", "ctx"), "tp"),
            P(("fsdp", "ctx"), "tp"),
            P("tp", ("fsdp", "ctx")),
            P(("fsdp", "ctx")),
            P(("fsdp", "ctx")),
            P(("fsdp", "ctx")),
            P(("fsdp", "ctx")),
            P("fsdp", None),
            P("fsdp", None),
            P("fsdp", "ctx", None),
        ),
        out_specs=(
            P("fsdp", "ctx", None),
            P("fsdp", "ctx", None),
            P(("fsdp", "ctx"), "tp"),
            P(("fsdp", "ctx"), "tp"),
            P(("fsdp", "ctx"), "tp"),
            P("tp", ("fsdp", "ctx")),
            P(("fsdp", "ctx"), "tp"),
            P(("fsdp", "ctx"), "tp"),
            P("tp", ("fsdp", "ctx")),
            P(("fsdp", "ctx")),
            P(("fsdp", "ctx")),
            P(("fsdp", "ctx")),
            P(("fsdp", "ctx")),
        ),
        check_vma=False,
    )
```

profile of v0, /device:TPU:0, one launch (start us, length us, event | category | flops | bytes accessed | tf_op | source)
XLA Modules:
  0.0 1594.3 jit_solution(6297504366629576011)
XLA Ops:
  14.2 25.8 %all-reduce.9 = (bf16[2304]{0:T(1024)(128)(2,1)S(1)}, bf16[2304]{0:T(1024)(128)(2,1)S(1)}, bf16[2304]{0:T(1024)(128)(2,1)S(1)}, bf16[2304]{0:T(1024)(128)(2,1)S(1)}) all-reduce(bf16[2304]{0:T(1024)(128)(2,1)S(1)} %dynamic-update-slice, bf16[2304]{0:T(1024)(128)(2,1)S(1)} %dynamic-update-slice.1, ...), channel_id=1, replica_groups=mesh['fsdp'=2,'ctx'=4,'tp'=4] {'fsdp','ctx'}, use_global_device_ids=true, to_apply=%add | all-reduce | flops 9216 | bytes 36864
  43.1 3.1 convolution_bitcast_fusion.1
  48.9 14.0 all-gather.15.cloned.1.call-done
  62.9 2.8 convolution_convert_fusion.8
  70.9 10.9 all-gather.27.cloned.1.call-done
  83.3 29.3 %all-gather.11.cloned.1.call-done = bf16[2304,512]{1,0:T(8,128)(2,1)} async-done(((bf16[288,512]{1,0:T(8,128)(2,1)}), bf16[2304,512]{1,0:T(8,128)(2,1)}) %all-gather.11.cloned.1.call-update) | async-done | bytes 2359312 | tf_op jit(solution)/shard_map/all_gather | solution.py:97
  112.6 4.3 copy.45
  116.9 3.2 fusion.81
  123.3 8.1 all-gather.17.cloned.1.call-done
  131.3 20.2 %while.39 = (s32[]{:T(128)}, bf16[2,512,256]{1,2,0:T(8,128)(2,1)}, f32[2,512]{1,0:T(2,128)S(1)}, s32[2,512]{1,0:T(2,128)S(1)}, s32[8,256]{1,0:T(8,128)S(1)}, /*i...) while((s32[]{:T(128)}, bf16[2,512,256]{1,2,0:T(8,128)(2,1)}, ...), condition=%wide.region_4.5_spmd.clone.clone.clone, body=%wide.region_1.4_spmd.clone.clone.sunk.clone | while | flops 1086364672 | bytes 32425128 | solution.py:143
  131.6 2.8 fusion.201
  137.1 4.3 fusion.203
  141.7 2.8 fusion.201
  147.2 4.3 fusion.203
  151.5 10.6 all-gather.19.cloned.1.call-done
  162.1 5.5 fusion.124
  169.8 169.9 %all-reduce.15.cloned.1.call-done = f32[512,2304]{1,0:T(8,128)} async-done(((f32[512,2304]{1,0:T(8,128)}), f32[512,2304]{1,0:T(8,128)}) %all-reduce.15.cloned.1.call-update) | async-done | bytes 4718608 | tf_op jit(solution)/shard_map/psum | solution.py:147
  339.7 2.9 multiply_reduce_fusion.7
  347.2 57.2 %all-gather.21.cloned.1.call-done = bf16[2304,2304]{1,0:T(8,128)(2,1)} async-done(((bf16[288,2304]{1,0:T(8,128)(2,1)}), bf16[2304,2304]{1,0:T(8,128)(2,1)}) %all-gather.21.cloned.1.call-update) | async-done | bytes 10616848 | tf_op jit(solution)/shard_map/all_gather | solution.py:150
  404.5 11.3 fusion.125
  415.7 54.5 %all-gather.23.cloned.1.call-done = bf16[2304,2304]{1,0:T(8,128)(2,1)} async-done(((bf16[288,2304]{1,0:T(8,128)(2,1)}), bf16[2304,2304]{1,0:T(8,128)(2,1)}) %all-gather.23.cloned.1.call-update) | async-done | bytes 10616848 | tf_op jit(solution)/shard_map/all_gather | solution.py:151
  470.2 12.5 multiply_convert_fusion.2
  482.7 53.1 %all-gather.25.cloned.1.call-done = bf16[2304,2304]{0,1:T(8,128)(2,1)} async-done(((bf16[2304,288]{0,1:T(8,128)(2,1)}), bf16[2304,2304]{0,1:T(8,128)(2,1)}) %all-gather.25.cloned.1.call-update) | async-done | bytes 10616848 | tf_op jit(solution)/shard_map/all_gather | solution.py:152
  535.8 11.7 fusion.126
  547.7 171.9 %all-reduce.17.cloned.1.call-done = f32[512,2304]{1,0:T(8,128)} async-done(((f32[512,2304]{1,0:T(8,128)}), f32[512,2304]{1,0:T(8,128)}) %all-reduce.17.cloned.1.call-update) | async-done | bytes 4718608 | tf_op jit(solution)/shard_map/psum | solution.py:160
  719.6 2.9 multiply_reduce_fusion.5
  725.3 5.3 fusion.56
  730.7 14.7 multiply_convert_fusion.1
  745.5 9.5 fusion.127
  754.9 12.2 convolution_add_fusion.4
  767.6 170.6 %all-reduce.19.cloned.1.call-done = f32[512,2304]{1,0:T(8,128)} async-done(((f32[512,2304]{1,0:T(8,128)}), f32[512,2304]{1,0:T(8,128)}) %all-reduce.19.cloned.1.call-update) | async-done | bytes 4718608 | tf_op jit(solution)/shard_map/psum | solution.py:175
  938.3 5.7 multiply_reduce_fusion.1
  944.0 6.3 multiply_reduce_fusion.2
  955.8 34.3 %while.40 = (s32[]{:T(128)}, f32[2048,256]{1,0:T(8,128)}, f32[2048,256]{1,0:T(8,128)}, f32[2,512,256]{1,2,0:T(8,128)}, s32[2,512]{1,0:T(2,128)S(1)}, /*index=5*/...) while((s32[]{:T(128)}, f32[2048,256]{1,0:T(8,128)}, ...), condition=%wide.region_16.17_spmd.clone.clone.clone.clone, body=%wide.region_14.16_spmd.clone.clone.clone.sunk.clone | while | flops 2717948928 | bytes 95113088 | solution.py:204
  959.9 2.8 multiply_convert_fusion.6
  962.8 3.2 convolution_add_fusion.9
  967.7 4.4 convolution_add_fusion.10
  976.4 2.8 multiply_convert_fusion.6
  979.2 3.9 convolution_add_fusion.9
  984.9 5.1 convolution_add_fusion.10
  990.0 2.9 copy.53
  995.5 3.0 convolution_convert_fusion.4
  998.6 4.9 convolution_convert_fusion.3
  1003.6 20.0 %reduce-scatter.10.cloned.1.call-done = f32[512,256]{0,1:T(8,128)} async-done(((f32[2048,256]{0,1:T(8,128)}), f32[512,256]{0,1:T(8,128)}) %reduce-scatter.10.cloned.1.call-update) | async-done | bytes 524304 | tf_op jit(solution)/shard_map/reduce_scatter | solution.py:208
  1023.6 2.3 fusion.100
  1028.0 29.6 %reduce-scatter.12.cloned.1.call-done = f32[512,256]{1,0:T(8,128)} async-done(((f32[2048,256]{1,0:T(8,128)}), f32[512,256]{1,0:T(8,128)}) %reduce-scatter.12.cloned.1.call-update) | async-done | bytes 524304 | tf_op jit(solution)/shard_map/reduce_scatter | solution.py:209
  1057.6 3.1 convolution_convert_fusion.5
  1066.8 10.6 convolution_convert_fusion
  1077.5 10.3 convolution_convert_fusion.2
  1087.8 10.6 convolution_convert_fusion.1
  1099.2 4.1 reduce-scatter.14.cloned.1.call-done
  1105.1 44.2 %reduce-scatter.20.cloned.1.call-done = bf16[512,288]{0,1:T(8,128)(2,1)} async-done(((bf16[512,2304]{0,1:T(8,128)(2,1)}), bf16[512,288]{0,1:T(8,128)(2,1)}) %reduce-scatter.20.cloned.1.call-update) | async-done | bytes 294928 | tf_op jit(solution)/shard_map/reduce_scatter | solution.py:242
  1151.2 38.0 %reduce-scatter.16.cloned.1.call-done = bf16[288,256]{1,0:T(8,128)(2,1)} async-done(((bf16[2304,256]{1,0:T(8,128)(2,1)}), bf16[288,256]{1,0:T(8,128)(2,1)}) %reduce-scatter.16.cloned.1.call-update) | async-done | bytes 147472 | tf_op jit(solution)/shard_map/reduce_scatter | solution.py:236
  1190.8 38.6 %reduce-scatter.18.cloned.1.call-done = bf16[288,256]{1,0:T(8,128)(2,1)} async-done(((bf16[2304,256]{1,0:T(8,128)(2,1)}), bf16[288,256]{1,0:T(8,128)(2,1)}) %reduce-scatter.18.cloned.1.call-update) | async-done | bytes 147472 | tf_op jit(solution)/shard_map/reduce_scatter | solution.py:239
  1231.1 96.9 %all-reduce.21.cloned.1.call-done = bf16[512,2304]{1,0:T(8,128)(2,1)} async-done(((bf16[512,2304]{1,0:T(8,128)(2,1)}), bf16[512,2304]{1,0:T(8,128)(2,1)}) %all-reduce.21.cloned.1.call-update) | async-done | bytes 2359312 | tf_op jit(solution)/shard_map/psum | solution.py:222
  1328.0 3.4 fusion.67
  1331.5 24.0 %all-reduce.8 = (bf16[2304]{0:T(1024)(128)(2,1)S(1)}, bf16[2304]{0:T(1024)(128)(2,1)S(1)}, bf16[2304]{0:T(1024)(128)(2,1)S(1)}, bf16[2304]{0:T(1024)(128)(2,1)S(1)}) all-reduce(bf16[2304]{0:T(1024)(128)(2,1)S(1)} %get-tuple-element.658, ...), channel_id=12, replica_groups=mesh['fsdp'=2,'ctx'=4,'tp'=4] {'fsdp','ctx'}, use_global_device_ids=true, to_apply=%region_29.30.clone | all-reduce | flops 9216 | bytes 36864
  1356.8 7.5 fusion.63
  1364.3 48.4 %reduce-scatter.26.cloned.1.call-done = bf16[2304,288]{0,1:T(8,128)(2,1)} async-done(((bf16[2304,2304]{0,1:T(8,128)(2,1)}), bf16[2304,288]{0,1:T(8,128)(2,1)}) %reduce-scatter.26.cloned.1.call-update) | async-done | bytes 1327120 | tf_op jit(solution)/shard_map/reduce_scatter | solution.py:257
  1412.7 3.0 convert_element_type.255
  1415.7 82.8 %reduce-scatter.22.cloned.1.call-done = bf16[288,2304]{1,0:T(8,128)(2,1)} async-done(((bf16[2304,2304]{1,0:T(8,128)(2,1)}), bf16[288,2304]{1,0:T(8,128)(2,1)}) %reduce-scatter.22.cloned.1.call-update) | async-done | bytes 1327120 | tf_op jit(solution)/shard_map/reduce_scatter | solution.py:251
  1498.5 3.0 convert_element_type.251
  1501.5 82.8 %reduce-scatter.24.cloned.1.call-done = bf16[288,2304]{1,0:T(8,128)(2,1)} async-done(((bf16[2304,2304]{1,0:T(8,128)(2,1)}), bf16[288,2304]{1,0:T(8,128)(2,1)}) %reduce-scatter.24.cloned.1.call-update) | async-done | bytes 1327120 | tf_op jit(solution)/shard_map/reduce_scatter | solution.py:254
  1584.2 3.0 convert_element_type.253
  (298 shorter events, 74.0 us)
Async XLA Ops:
  7.2 36.0 %all-gather.13.cloned.1.call-start = ((), (), s32[]{:S(2)}) async-start(), calls=%async_computation.10 | async-start | bytes 1327104 | tf_op jit(solution)/shard_map/all_gather | solution.py:98
  7.9 55.0 %all-gather.15.cloned.1.call-start = ((), (), s32[]{:S(2)}) async-start(), calls=%async_computation.11 | async-start | bytes 1327104 | tf_op jit(solution)/shard_map/all_gather | solution.py:99
  8.7 73.1 %all-gather.27.cloned.1.call-start = ((), (), s32[]{:S(2)}) async-start(), calls=%async_computation.30 | async-start | bytes 1310720 | tf_op jit(solution)/shard_map/all_gather | solution.py:124
  40.0 76.8 %copy-start.31 = (f32[2304]{0:T(1024)}, f32[2304]{0:T(1024)S(1)}, u32[]{:S(2)}) copy-start(f32[2304]{0:T(1024)S(1)} %convert_element_type.212) | copy-start | bytes 27652
  40.8 25.6 %copy-start.45 = (f32[128]{0:T(128)}, f32[128]{0:T(128)S(1)}, u32[]{:S(2)}) copy-start(f32[128]{0:T(128)S(1)} %multiply_power_fusion) | copy-start | bytes 1540
  40.9 25.5 %copy-start.35 = (f32[512]{0:T(512)}, f32[512]{0:T(512)S(1)}, u32[]{:S(2)}) copy-start(f32[512]{0:T(512)S(1)} %get-tuple-element.717) | copy-start | bytes 6148
  43.1 19.8 %copy-start.7 = (bf16[1,512,2304]{2,1,0:T(8,128)(2,1)S(1)}, bf16[1,512,2304]{2,1,0:T(8,128)(2,1)}, u32[]{:S(2)}) copy-start(bf16[1,512,2304]{2,1,0:T(8,128)(2,1)} %param.19) | copy-start | bytes 7077892
  43.1 73.8 %copy-start.42 = (f32[512]{0:T(512)}, f32[512]{0:T(512)S(1)}, u32[]{:S(2)}) copy-start(f32[512]{0:T(512)S(1)} %add_rsqrt_fusion.3) | copy-start | bytes 6148
  48.2 64.4 %all-gather.11.cloned.1.call-start = ((), (), s32[]{:S(2)}) async-start(), calls=%async_computation.9 | async-start | bytes 2654208 | tf_op jit(solution)/shard_map/all_gather | solution.py:97
  48.8 19.4 %copy-start.49 = (s32[1,8]{1,0:T(1,128)S(1)}, s32[1,8]{1,0:T(1,128)}, u32[]{:S(2)}) copy-start(s32[1,8]{1,0:T(1,128)} %param.32) | copy-start | bytes 100
  48.8 20.7 %copy-start.44 = (s32[1,2048]{1,0:T(1,128)S(1)}, s32[1,2048]{1,0:T(1,128)}, u32[]{:S(2)}) copy-start(s32[1,2048]{1,0:T(1,128)} %param.31) | copy-start | bytes 24580
  48.8 82.5 %all-gather.17.cloned.1.call-start = ((), (), s32[]{:S(2)}) async-start(), calls=%async_computation.12 | async-start | bytes 1310720 | tf_op jit(solution)/shard_map/all_gather | solution.py:125
  65.7 96.4 %all-gather.19.cloned.1.call-start = ((), (), s32[]{:S(2)}) async-start(), calls=%async_computation.13 | async-start | bytes 2654208 | tf_op jit(solution)/shard_map/all_gather | solution.py:100
  66.3 273.4 %all-reduce.15.cloned.1.call-start = ((), (), s32[]{:S(2)}) async-start(), calls=%async_computation.14 | async-start | bytes 9437184 | tf_op jit(solution)/shard_map/psum | solution.py:147
  116.9 3.2 copy-start.13
  116.9 3.3 copy-start.15
  151.5 16.1 %copy-start.27 = (s32[2,512]{1,0:T(2,128)}, s32[2,512]{1,0:T(2,128)S(1)}, u32[]{:S(2)}) copy-start(s32[2,512]{1,0:T(2,128)S(1)} %get-tuple-element.1139) | copy-start | bytes 12292
  151.5 16.1 %copy-start.29 = (s32[2,512]{1,0:T(2,128)}, s32[2,512]{1,0:T(2,128)S(1)}, u32[]{:S(2)}) copy-start(s32[2,512]{1,0:T(2,128)S(1)} %get-tuple-element.1140) | copy-start | bytes 12292
  151.5 16.1 %copy-start.33 = (s32[8]{0:T(128)}, s32[8]{0:T(128)S(1)}, u32[]{:S(2)}) copy-start(s32[8]{0:T(128)S(1)} %get-tuple-element.1145) | copy-start | bytes 100
  151.5 16.1 %copy-start.37 = (f32[2,512]{1,0:T(2,128)}, f32[2,512]{1,0:T(2,128)S(1)}, u32[]{:S(2)}) copy-start(f32[2,512]{1,0:T(2,128)S(1)} %get-tuple-element.1028) | copy-start | bytes 12292
  167.7 236.8 %all-gather.21.cloned.1.call-start = ((), (), s32[]{:S(2)}) async-start(), calls=%async_computation.15 | async-start | bytes 11943936 | tf_op jit(solution)/shard_map/all_gather | solution.py:150
  168.4 301.8 %all-gather.23.cloned.1.call-start = ((), (), s32[]{:S(2)}) async-start(), calls=%async_computation.16 | async-start | bytes 11943936 | tf_op jit(solution)/shard_map/all_gather | solution.py:151
  169.1 366.6 %all-gather.25.cloned.1.call-start = ((), (), s32[]{:S(2)}) async-start(), calls=%async_computation.17 | async-start | bytes 11943936 | tf_op jit(solution)/shard_map/all_gather | solution.py:152
  169.7 549.8 %all-reduce.17.cloned.1.call-start = ((), (), s32[]{:S(2)}) async-start(), calls=%async_computation.18 | async-start | bytes 9437184 | tf_op jit(solution)/shard_map/psum | solution.py:160
  339.7 3.8 copy-start.4
  347.2 123.0 %copy-start.17 = (bf16[512,2304]{1,0:T(8,128)(2,1)}, bf16[512,2304]{1,0:T(8,128)(2,1)S(1)}, u32[]{:S(2)}) copy-start(bf16[512,2304]{1,0:T(8,128)(2,1)S(1)} %multiply_convert_fusion.3) | copy-start | bytes 7077892
  547.4 175.0 %copy-start.9 = (bf16[1,512,2304]{2,1,0:T(8,128)(2,1)S(1)}, bf16[1,512,2304]{2,1,0:T(8,128)(2,1)}, u32[]{:S(2)}) copy-start(bf16[1,512,2304]{2,1,0:T(8,128)(2,1)} %param.33) | copy-start | bytes 7077892
  547.5 390.8 %all-reduce.19.cloned.1.call-start = ((), (), s32[]{:S(2)}) async-start(), calls=%async_computation.19 | async-start | bytes 9437184 | tf_op jit(solution)/shard_map/psum | solution.py:175
  719.6 3.8 copy-start.5
  723.3 7.3 slice-start.5
  725.3 5.4 slice-start.6
  725.3 20.1 %slice-start.2 = ((s8[10616832]{0:T(1024)(128)(4,1)}), s8[4194304]{0:T(1024)(128)(4,1)S(1)}, s32[]{:S(2)}) async-start(s8[10616832]{0:T(1024)(128)(4,1)} %bitcast.324), calls=%async_computation.33 | async-start | bytes 8388608
  730.7 14.8 copy-start.12
  730.7 14.8 slice-start.3
  730.7 14.8 slice-start.4
  745.4 9.5 copy-start.50
  767.2 256.4 %reduce-scatter.10.cloned.1.call-start = ((), (), s32[]{:S(2)}) async-start(), calls=%async_computation.20 | async-start | bytes 2621440 | tf_op jit(solution)/shard_map/reduce_scatter | solution.py:208
  938.3 5.7 copy-start.10
  938.3 12.0 slice-start
  944.0 6.3 slice-start.1
  950.3 3.4 copy-start.18
  955.8 4.2 copy-start.25
  962.8 4.9 copy-start.1
  967.7 4.4 copy-start.26
  967.7 4.4 copy-start.48
  972.2 4.2 copy-start.25
  979.2 3.9 copy-start.22
  979.2 5.7 copy-start.1
  984.9 5.2 copy-start.26
  984.9 5.2 copy-start.48
  993.0 64.5 %reduce-scatter.12.cloned.1.call-start = ((), (), s32[]{:S(2)}) async-start(), calls=%async_computation.21 | async-start | bytes 2621440 | tf_op jit(solution)/shard_map/reduce_scatter | solution.py:209
  993.6 109.7 %reduce-scatter.14.cloned.1.call-start = ((), (), s32[]{:S(2)}) async-start(), calls=%async_computation.23 | async-start | bytes 2654208 | tf_op jit(solution)/shard_map/reduce_scatter | solution.py:233
  998.6 25.0 %copy-start.36 = (f32[512]{0:T(512)S(1)}, f32[512]{0:T(512)}, u32[]{:S(2)}) copy-start(f32[512]{0:T(512)} %copy-done.35) | copy-start | bytes 6148
  998.6 25.0 %copy-start.46 = (f32[128]{0:T(128)S(1)}, f32[128]{0:T(128)}, u32[]{:S(2)}) copy-start(f32[128]{0:T(128)} %copy-done.45) | copy-start | bytes 1540
  998.6 150.7 %reduce-scatter.20.cloned.1.call-start = ((), (), s32[]{:S(2)}) async-start(), calls=%async_computation.26 | async-start | bytes 2654208 | tf_op jit(solution)/shard_map/reduce_scatter | solution.py:242
  1003.5 185.7 %reduce-scatter.16.cloned.1.call-start = ((), (), s32[]{:S(2)}) async-start(), calls=%async_computation.24 | async-start | bytes 1327104 | tf_op jit(solution)/shard_map/reduce_scatter | solution.py:236
  1027.9 201.5 %reduce-scatter.18.cloned.1.call-start = ((), (), s32[]{:S(2)}) async-start(), calls=%async_computation.25 | async-start | bytes 1327104 | tf_op jit(solution)/shard_map/reduce_scatter | solution.py:239
  1060.7 267.4 %all-reduce.21.cloned.1.call-start = ((), (), s32[]{:S(2)}) async-start(), calls=%async_computation.22 | async-start | bytes 4718592 | tf_op jit(solution)/shard_map/psum | solution.py:222
  1066.7 346.0 %reduce-scatter.26.cloned.1.call-start = ((), (), s32[]{:S(2)}) async-start(), calls=%async_computation.29 | async-start | bytes 11943936 | tf_op jit(solution)/shard_map/reduce_scatter | solution.py:257
  1077.4 421.0 %reduce-scatter.22.cloned.1.call-start = ((), (), s32[]{:S(2)}) async-start(), calls=%async_computation.27 | async-start | bytes 11943936 | tf_op jit(solution)/shard_map/reduce_scatter | solution.py:251
  1087.8 496.4 %reduce-scatter.24.cloned.1.call-start = ((), (), s32[]{:S(2)}) async-start(), calls=%async_computation.28 | async-start | bytes 11943936 | tf_op jit(solution)/shard_map/reduce_scatter | solution.py:254
  1098.5 233.0 %copy-start.39 = (bf16[2304]{0:T(1024)(128)(2,1)S(1)}, bf16[2304]{0:T(1024)(128)(2,1)}, u32[]{:S(2)}) copy-start(bf16[2304]{0:T(1024)(128)(2,1)} %get-tuple-element.654) | copy-start | bytes 13828
  1098.5 233.0 %copy-start.40 = (bf16[2304]{0:T(1024)(128)(2,1)S(1)}, bf16[2304]{0:T(1024)(128)(2,1)}, u32[]{:S(2)}) copy-start(bf16[2304]{0:T(1024)(128)(2,1)} %get-tuple-element.656) | copy-start | bytes 13828
  1098.5 233.0 %copy-start.41 = (bf16[2304]{0:T(1024)(128)(2,1)S(1)}, bf16[2304]{0:T(1024)(128)(2,1)}, u32[]{:S(2)}) copy-start(bf16[2304]{0:T(1024)(128)(2,1)} %get-tuple-element.652) | copy-start | bytes 13828
  (24 other events, 49.0 us)
Sparse Core Ops, SparseCore 0:
  9.9 26.9 all-gather.12
  38.7 24.1 all-gather.14
  65.1 16.7 all-gather.26
  83.5 29.0 all-gather.10
  114.6 16.7 all-gather.16
  133.1 29.0 all-gather.18
  167.7 171.9 all-reduce.14
  341.6 62.7 all-gather.20
  406.3 63.8 all-gather.22
  471.9 63.8 all-gather.24
  547.6 171.9 all-reduce.16
  767.3 170.9 all-reduce.18
  993.1 30.4 reduce-scatter.9
  1026.1 31.3 reduce-scatter.11
  1060.7 42.4 reduce-scatter.13
  1106.8 42.4 reduce-scatter.19
  1152.4 36.7 reduce-scatter.15
  1192.6 36.7 reduce-scatter.17
  1232.4 95.5 all-reduce.20
  1331.4 81.2 reduce-scatter.25
  1416.2 82.2 reduce-scatter.21
  1502.0 82.1 reduce-scatter.23
where the time goes:
time: 1600 us; the launch traced here: 1590 us
  waiting for transfers between devices  1240 us (78%)
  matrix products  179 us (11%)
  other arithmetic  77.3 us (5%)
  blocking collectives  49.8 us (3%)
  local copies, waits for them, and re-layouts  29.6 us (2%)
  between operations  16.7 us (1%)
    psum x1, waiting for transfers between devices, per_device(): lax.psum(jnp.dot(activ, down_full, preferred_element_type=jnp.float32), '...  172 us
    psum x1, waiting for transfers between devices, per_device(): lax.psum(times_transposed(d_gate_low, gate_full) + times_transposed(d_up_...  171 us
    psum x1, waiting for transfers between devices, per_device(): lax.psum(jnp.dot(attended, out_full, preferred_element_type=jnp.float32),...  170 us
    psum x1, waiting for transfers between devices, per_device(): lax.psum((times_transposed(d_q_lin, q_full) + times_transposed(d_key_lin,...  96.9 us
    reduce_scatter x1, waiting for transfers between devices, per_device(): lax.psum_scatter(grad_gate.astype(jnp.bfloat16), ('fsdp', 'ctx'), scatter...  82.8 us
    reduce_scatter x1, waiting for transfers between devices, per_device(): lax.psum_scatter(grad_up.astype(jnp.bfloat16), ('fsdp', 'ctx'), scatter_d...  82.8 us
    all_gather x1, waiting for transfers between devices, per_device(): lax.all_gather(gate_weight, ('fsdp', 'ctx'), axis=0, tiled=True)  57.2 us
    all_gather x1, waiting for transfers between devices, per_device(): lax.all_gather(up_weight, ('fsdp', 'ctx'), axis=0, tiled=True)  54.5 us
  transfers between devices with their start and end apart: 22, of which 21 were waited for; matrix products, arithmetic and copies ran while one was open for 10% of the time, Pallas kernels for 0%

commit v1 on v0

--- a/solution.py
+++ b/solution.py
@@ -144,7 +144,10 @@
     attended = (
         outputs.transpose(1, 0, 2).reshape(tok_count, heads_local * HEAD_DIM).astype(jnp.bfloat16)
     )
-    branch_attn = lax.psum(jnp.dot(attended, out_full, preferred_element_type=jnp.float32), "tp")
+    branch_attn = jnp.sum(
+        lax.all_gather(jnp.dot(attended, out_full, preferred_element_type=jnp.float32), "tp"),
+        axis=0,
+    )
     resid = inputs + normalize(branch_attn, gain_two)
     gate_full, up_full, down_full, gain_three, gain_four = (
         lax.all_gather(gate_weight, ("fsdp", "ctx"), axis=0, tiled=True),

time: 1600 us -> 1760 us (1.10)
  waiting for transfers between devices: 1240 us -> 1380 us
    all_gather x0 -> x1, waiting for transfers between devices: none -> 321 us  [per_device(): lax.all_gather(jnp.dot(attended, out_full, preferred_element_type=jnp.flo...]
    psum x1 -> x0, waiting for transfers between devices: 170 us -> none  [per_device(): lax.psum(jnp.dot(attended, out_full, preferred_element_type=jnp.float32),...]
where the time goes in v1:
time: 1760 us; the launch traced here: 1750 us
  waiting for transfers between devices  1380 us (78%)
  matrix products  178 us (10%)
  other arithmetic  87.7 us (5%)
  blocking collectives  49.8 us (3%)
  local copies, waits for them, and re-layouts  30.1 us (2%)
    all_gather x1, waiting for transfers between devices, per_device(): lax.all_gather(jnp.dot(attended, out_full, preferred_element_type=jnp.flo...  321 us
    psum x1, waiting for transfers between devices, per_device(): lax.psum(jnp.dot(activ, down_full, preferred_element_type=jnp.float32), '...  172 us
    psum x1, waiting for transfers between devices, per_device(): lax.psum(times_transposed(d_gate_low, gate_full) + times_transposed(d_up_...  171 us
    psum x1, waiting for transfers between devices, per_device(): lax.psum((times_transposed(d_q_lin, q_full) + times_transposed(d_key_lin,...  96.9 us
    reduce_scatter x1, waiting for transfers between devices, per_device(): lax.psum_scatter(grad_gate.astype(jnp.bfloat16), ('fsdp', 'ctx'), scatter...  82.8 us
    reduce_scatter x1, waiting for transfers between devices, per_device(): lax.psum_scatter(grad_up.astype(jnp.bfloat16), ('fsdp', 'ctx'), scatter_d...  82.8 us
    all_gather x1, waiting for transfers between devices, per_device(): lax.all_gather(up_weight, ('fsdp', 'ctx'), axis=0, tiled=True)  54.5 us
    all_gather x1, waiting for transfers between devices, per_device(): lax.all_gather(down_weight, ('fsdp', 'ctx'), axis=1, tiled=True)  53.1 us
  transfers between devices with their start and end apart: 22, of which 21 were waited for; matrix products, arithmetic and copies ran while one was open for 10% of the time, Pallas kernels for 0%

profile of v1, /device:TPU:0, one launch (start us, length us, event | category | flops | bytes accessed | tf_op | source)
XLA Modules:
  0.0 1746.1 jit_solution(7621023788022729259)
XLA Ops:
  14.2 25.8 %all-reduce.9 = (bf16[2304]{0:T(1024)(128)(2,1)S(1)}, bf16[2304]{0:T(1024)(128)(2,1)S(1)}, bf16[2304]{0:T(1024)(128)(2,1)S(1)}, bf16[2304]{0:T(1024)(128)(2,1)S(1)}) all-reduce(bf16[2304]{0:T(1024)(128)(2,1)S(1)} %dynamic-update-slice, bf16[2304]{0:T(1024)(128)(2,1)S(1)} %dynamic-update-slice.1, ...), channel_id=1, replica_groups=mesh['fsdp'=2,'ctx'=4,'tp'=4] {'fsdp','ctx'}, use_global_device_ids=true, to_apply=%add | all-reduce | flops 9216 | bytes 36864
  43.1 3.1 convolution_bitcast_fusion.1
  48.9 14.0 all-gather.17.cloned.1.call-done
  62.9 2.8 convolution_convert_fusion.8
  70.9 10.9 all-gather.29.cloned.1.call-done
  83.3 29.3 %all-gather.13.cloned.1.call-done = bf16[2304,512]{1,0:T(8,128)(2,1)} async-done(((bf16[288,512]{1,0:T(8,128)(2,1)}), bf16[2304,512]{1,0:T(8,128)(2,1)}) %all-gather.13.cloned.1.call-update) | async-done | bytes 2359312 | tf_op jit(solution)/shard_map/all_gather | solution.py:97
  112.6 4.3 copy.45
  116.9 3.2 fusion.81
  123.3 8.1 all-gather.19.cloned.1.call-done
  131.3 20.2 %while.39 = (s32[]{:T(128)}, bf16[2,512,256]{1,2,0:T(8,128)(2,1)}, f32[2,512]{1,0:T(2,128)S(1)}, s32[2,512]{1,0:T(2,128)S(1)}, s32[8,256]{1,0:T(8,128)S(1)}, /*i...) while((s32[]{:T(128)}, bf16[2,512,256]{1,2,0:T(8,128)(2,1)}, ...), condition=%wide.region_4.5_spmd.clone.clone.clone, body=%wide.region_1.4_spmd.clone.clone.sunk.clone | while | flops 1086364672 | bytes 32425128 | solution.py:143
  131.6 2.8 fusion.201
  137.1 4.3 fusion.203
  141.7 2.8 fusion.201
  147.2 4.3 fusion.203
  151.5 10.6 all-gather.21.cloned.1.call-done
  162.1 5.5 fusion.124
  169.8 320.5 %all-gather.31.cloned.1.call-done = f32[2048,2304]{1,0:T(8,128)} async-done(((f32[512,2304]{1,0:T(8,128)}), f32[2048,2304]{1,0:T(8,128)}) %all-gather.31.cloned.1.call-update) | async-done | bytes 18874384 | tf_op jit(solution)/shard_map/all_gather | solution.py:148
  490.4 10.3 reduce_sum.160
  500.7 2.9 multiply_reduce_fusion.7
  508.4 46.6 %all-gather.23.cloned.1.call-done = bf16[2304,2304]{1,0:T(8,128)(2,1)} async-done(((bf16[288,2304]{1,0:T(8,128)(2,1)}), bf16[2304,2304]{1,0:T(8,128)(2,1)}) %all-gather.23.cloned.1.call-update) | async-done | bytes 10616848 | tf_op jit(solution)/shard_map/all_gather | solution.py:153
  554.9 11.2 fusion.125
  566.2 54.5 %all-gather.25.cloned.1.call-done = bf16[2304,2304]{1,0:T(8,128)(2,1)} async-done(((bf16[288,2304]{1,0:T(8,128)(2,1)}), bf16[2304,2304]{1,0:T(8,128)(2,1)}) %all-gather.25.cloned.1.call-update) | async-done | bytes 10616848 | tf_op jit(solution)/shard_map/all_gather | solution.py:154
  620.7 12.5 multiply_convert_fusion.2
  633.2 53.1 %all-gather.27.cloned.1.call-done = bf16[2304,2304]{0,1:T(8,128)(2,1)} async-done(((bf16[2304,288]{0,1:T(8,128)(2,1)}), bf16[2304,2304]{0,1:T(8,128)(2,1)}) %all-gather.27.cloned.1.call-update) | async-done | bytes 10616848 | tf_op jit(solution)/shard_map/all_gather | solution.py:155
  686.3 11.7 fusion.126
  698.4 171.6 %all-reduce.14.cloned.1.call-done = f32[512,2304]{1,0:T(8,128)} async-done(((f32[512,2304]{1,0:T(8,128)}), f32[512,2304]{1,0:T(8,128)}) %all-reduce.14.cloned.1.call-update) | async-done | bytes 4718608 | tf_op jit(solution)/shard_map/psum | solution.py:163
  870.1 2.9 multiply_reduce_fusion.5
  875.8 5.3 fusion.56
  881.2 14.7 multiply_convert_fusion.1
  896.0 9.4 fusion.127
  905.4 12.2 convolution_add_fusion.4
  917.7 171.0 %all-reduce.16.cloned.1.call-done = f32[512,2304]{1,0:T(8,128)} async-done(((f32[512,2304]{1,0:T(8,128)}), f32[512,2304]{1,0:T(8,128)}) %all-reduce.16.cloned.1.call-update) | async-done | bytes 4718608 | tf_op jit(solution)/shard_map/psum | solution.py:178
  1088.8 5.7 multiply_reduce_fusion.1
  1094.5 6.3 multiply_reduce_fusion.2
  1106.6 34.5 %while.40 = (s32[]{:T(128)}, f32[2048,256]{1,0:T(8,128)}, f32[2048,256]{1,0:T(8,128)}, f32[2,512,256]{1,2,0:T(8,128)}, s32[2,512]{1,0:T(2,128)S(1)}, /*index=5*/...) while((s32[]{:T(128)}, f32[2048,256]{1,0:T(8,128)}, ...), condition=%wide.region_16.17_spmd.clone.clone.clone.clone, body=%wide.region_14.16_spmd.clone.clone.clone.sunk.clone | while | flops 2717948928 | bytes 95113088 | solution.py:207
  1110.9 2.8 multiply_convert_fusion.6
  1113.8 3.2 convolution_add_fusion.9
  1118.8 4.4 convolution_add_fusion.10
  1127.4 2.8 multiply_convert_fusion.6
  1130.2 3.9 convolution_add_fusion.9
  1135.9 5.1 convolution_add_fusion.10
  1141.0 2.9 copy.53
  1146.5 3.0 convolution_convert_fusion.4
  1149.6 4.8 convolution_convert_fusion.3
  1154.6 20.0 %reduce-scatter.10.cloned.1.call-done = f32[512,256]{0,1:T(8,128)} async-done(((f32[2048,256]{0,1:T(8,128)}), f32[512,256]{0,1:T(8,128)}) %reduce-scatter.10.cloned.1.call-update) | async-done | bytes 524304 | tf_op jit(solution)/shard_map/reduce_scatter | solution.py:211
  1179.0 29.6 %reduce-scatter.12.cloned.1.call-done = f32[512,256]{1,0:T(8,128)} async-done(((f32[2048,256]{1,0:T(8,128)}), f32[512,256]{1,0:T(8,128)}) %reduce-scatter.12.cloned.1.call-update) | async-done | bytes 524304 | tf_op jit(solution)/shard_map/reduce_scatter | solution.py:212
  1208.6 3.1 convolution_convert_fusion.5
  1217.8 10.5 convolution_convert_fusion
  1228.4 10.3 convolution_convert_fusion.2
  1238.8 10.6 convolution_convert_fusion.1
  1250.2 4.8 reduce-scatter.14.cloned.1.call-done
  1256.8 44.2 %reduce-scatter.20.cloned.1.call-done = bf16[512,288]{0,1:T(8,128)(2,1)} async-done(((bf16[512,2304]{0,1:T(8,128)(2,1)}), bf16[512,288]{0,1:T(8,128)(2,1)}) %reduce-scatter.20.cloned.1.call-update) | async-done | bytes 294928 | tf_op jit(solution)/shard_map/reduce_scatter | solution.py:245
  1302.8 38.1 %reduce-scatter.16.cloned.1.call-done = bf16[288,256]{1,0:T(8,128)(2,1)} async-done(((bf16[2304,256]{1,0:T(8,128)(2,1)}), bf16[288,256]{1,0:T(8,128)(2,1)}) %reduce-scatter.16.cloned.1.call-update) | async-done | bytes 147472 | tf_op jit(solution)/shard_map/reduce_scatter | solution.py:239
  1342.5 38.6 %reduce-scatter.18.cloned.1.call-done = bf16[288,256]{1,0:T(8,128)(2,1)} async-done(((bf16[2304,256]{1,0:T(8,128)(2,1)}), bf16[288,256]{1,0:T(8,128)(2,1)}) %reduce-scatter.18.cloned.1.call-update) | async-done | bytes 147472 | tf_op jit(solution)/shard_map/reduce_scatter | solution.py:242
  1382.8 96.9 %all-reduce.18.cloned.1.call-done = bf16[512,2304]{1,0:T(8,128)(2,1)} async-done(((bf16[512,2304]{1,0:T(8,128)(2,1)}), bf16[512,2304]{1,0:T(8,128)(2,1)}) %all-reduce.18.cloned.1.call-update) | async-done | bytes 2359312 | tf_op jit(solution)/shard_map/psum | solution.py:225
  1479.7 3.4 fusion.67
  1483.2 24.0 %all-reduce.8 = (bf16[2304]{0:T(1024)(128)(2,1)S(1)}, bf16[2304]{0:T(1024)(128)(2,1)S(1)}, bf16[2304]{0:T(1024)(128)(2,1)S(1)}, bf16[2304]{0:T(1024)(128)(2,1)S(1)}) all-reduce(bf16[2304]{0:T(1024)(128)(2,1)S(1)} %get-tuple-element.658, ...), channel_id=13, replica_groups=mesh['fsdp'=2,'ctx'=4,'tp'=4] {'fsdp','ctx'}, use_global_device_ids=true, to_apply=%region_29.30.clone | all-reduce | flops 9216 | bytes 36864
  1508.5 7.5 fusion.63
  1516.0 48.4 %reduce-scatter.26.cloned.1.call-done = bf16[2304,288]{0,1:T(8,128)(2,1)} async-done(((bf16[2304,2304]{0,1:T(8,128)(2,1)}), bf16[2304,288]{0,1:T(8,128)(2,1)}) %reduce-scatter.26.cloned.1.call-update) | async-done | bytes 1327120 | tf_op jit(solution)/shard_map/reduce_scatter | solution.py:260
  1564.4 3.0 convert_element_type.255
  1567.4 82.8 %reduce-scatter.22.cloned.1.call-done = bf16[288,2304]{1,0:T(8,128)(2,1)} async-done(((bf16[2304,2304]{1,0:T(8,128)(2,1)}), bf16[288,2304]{1,0:T(8,128)(2,1)}) %reduce-scatter.22.cloned.1.call-update) | async-done | bytes 1327120 | tf_op jit(solution)/shard_map/reduce_scatter | solution.py:254
  1650.1 3.0 convert_element_type.251
  1653.1 82.8 %reduce-scatter.24.cloned.1.call-done = bf16[288,2304]{1,0:T(8,128)(2,1)} async-done(((bf16[2304,2304]{1,0:T(8,128)(2,1)}), bf16[288,2304]{1,0:T(8,128)(2,1)}) %reduce-scatter.24.cloned.1.call-update) | async-done | bytes 1327120 | tf_op jit(solution)/shard_map/reduce_scatter | solution.py:257
  1735.9 3.0 convert_element_type.253
  (307 shorter events, 76.7 us)
Async XLA Ops:
  7.2 36.0 %all-gather.15.cloned.1.call-start = ((), (), s32[]{:S(2)}) async-start(), calls=%async_computation.10 | async-start | bytes 1327104 | tf_op jit(solution)/shard_map/all_gather | solution.py:98
  7.9 55.0 %all-gather.17.cloned.1.call-start = ((), (), s32[]{:S(2)}) async-start(), calls=%async_computation.11 | async-start | bytes 1327104 | tf_op jit(solution)/shard_map/all_gather | solution.py:99
  8.7 73.2 %all-gather.29.cloned.1.call-start = ((), (), s32[]{:S(2)}) async-start(), calls=%async_computation.29 | async-start | bytes 1310720 | tf_op jit(solution)/shard_map/all_gather | solution.py:124
  40.0 76.8 %copy-start.35 = (f32[2304]{0:T(1024)}, f32[2304]{0:T(1024)S(1)}, u32[]{:S(2)}) copy-start(f32[2304]{0:T(1024)S(1)} %convert_element_type.212) | copy-start | bytes 27652
  40.8 25.6 %copy-start.49 = (f32[128]{0:T(128)}, f32[128]{0:T(128)S(1)}, u32[]{:S(2)}) copy-start(f32[128]{0:T(128)S(1)} %multiply_power_fusion) | copy-start | bytes 1540
  40.9 25.5 %copy-start.39 = (f32[512]{0:T(512)}, f32[512]{0:T(512)S(1)}, u32[]{:S(2)}) copy-start(f32[512]{0:T(512)S(1)} %get-tuple-element.717) | copy-start | bytes 6148
  43.1 19.8 %copy-start.7 = (bf16[1,512,2304]{2,1,0:T(8,128)(2,1)S(1)}, bf16[1,512,2304]{2,1,0:T(8,128)(2,1)}, u32[]{:S(2)}) copy-start(bf16[1,512,2304]{2,1,0:T(8,128)(2,1)} %param.19) | copy-start | bytes 7077892
  43.1 73.8 %copy-start.46 = (f32[512]{0:T(512)}, f32[512]{0:T(512)S(1)}, u32[]{:S(2)}) copy-start(f32[512]{0:T(512)S(1)} %add_rsqrt_fusion.3) | copy-start | bytes 6148
  48.2 64.4 %all-gather.13.cloned.1.call-start = ((), (), s32[]{:S(2)}) async-start(), calls=%async_computation.9 | async-start | bytes 2654208 | tf_op jit(solution)/shard_map/all_gather | solution.py:97
  48.8 19.4 %copy-start.53 = (s32[1,8]{1,0:T(1,128)S(1)}, s32[1,8]{1,0:T(1,128)}, u32[]{:S(2)}) copy-start(s32[1,8]{1,0:T(1,128)} %param.32) | copy-start | bytes 100
  48.8 20.7 %copy-start.48 = (s32[1,2048]{1,0:T(1,128)S(1)}, s32[1,2048]{1,0:T(1,128)}, u32[]{:S(2)}) copy-start(s32[1,2048]{1,0:T(1,128)} %param.31) | copy-start | bytes 24580
  48.8 82.5 %all-gather.19.cloned.1.call-start = ((), (), s32[]{:S(2)}) async-start(), calls=%async_computation.12 | async-start | bytes 1310720 | tf_op jit(solution)/shard_map/all_gather | solution.py:125
  65.7 96.4 %all-gather.21.cloned.1.call-start = ((), (), s32[]{:S(2)}) async-start(), calls=%async_computation.13 | async-start | bytes 2654208 | tf_op jit(solution)/shard_map/all_gather | solution.py:100
  66.3 424.1 %all-gather.31.cloned.1.call-start = ((), (), s32[]{:S(2)}) async-start(), calls=%async_computation.30 | async-start | bytes 23592960 | tf_op jit(solution)/shard_map/all_gather | solution.py:148
  151.5 16.1 copy-start.9
  151.5 16.1 copy-start.24
  151.5 16.1 copy-start.31
  151.5 16.1 copy-start.33
  151.5 16.1 copy-start.37
  151.5 16.1 copy-start.41
  167.7 387.3 %all-gather.23.cloned.1.call-start = ((), (), s32[]{:S(2)}) async-start(), calls=%async_computation.14 | async-start | bytes 11943936 | tf_op jit(solution)/shard_map/all_gather | solution.py:153
  168.4 452.3 %all-gather.25.cloned.1.call-start = ((), (), s32[]{:S(2)}) async-start(), calls=%async_computation.15 | async-start | bytes 11943936 | tf_op jit(solution)/shard_map/all_gather | solution.py:154
  169.2 517.1 %all-gather.27.cloned.1.call-start = ((), (), s32[]{:S(2)}) async-start(), calls=%async_computation.16 | async-start | bytes 11943936 | tf_op jit(solution)/shard_map/all_gather | solution.py:155
  169.8 700.3 %all-reduce.14.cloned.1.call-start = ((), (), s32[]{:S(2)}) async-start(), calls=%async_computation.17 | async-start | bytes 9437184 | tf_op jit(solution)/shard_map/psum | solution.py:163
  500.7 3.9 copy-start.2
  508.4 112.3 %copy-start.19 = (bf16[512,2304]{1,0:T(8,128)(2,1)}, bf16[512,2304]{1,0:T(8,128)(2,1)S(1)}, u32[]{:S(2)}) copy-start(bf16[512,2304]{1,0:T(8,128)(2,1)S(1)} %multiply_convert_fusion.3) | copy-start | bytes 7077892
  697.9 175.0 %copy-start.11 = (bf16[1,512,2304]{2,1,0:T(8,128)(2,1)S(1)}, bf16[1,512,2304]{2,1,0:T(8,128)(2,1)}, u32[]{:S(2)}) copy-start(bf16[1,512,2304]{2,1,0:T(8,128)(2,1)} %param.33) | copy-start | bytes 7077892
  698.0 390.8 %all-reduce.16.cloned.1.call-start = ((), (), s32[]{:S(2)}) async-start(), calls=%async_computation.18 | async-start | bytes 9437184 | tf_op jit(solution)/shard_map/psum | solution.py:178
  870.1 3.8 copy-start.5
  873.8 7.4 slice-start.5
  875.8 5.4 slice-start.6
  875.8 20.1 %slice-start.2 = ((s8[10616832]{0:T(1024)(128)(4,1)}), s8[4194304]{0:T(1024)(128)(4,1)S(1)}, s32[]{:S(2)}) async-start(s8[10616832]{0:T(1024)(128)(4,1)} %bitcast.326), calls=%async_computation.33 | async-start | bytes 8388608
  881.2 14.8 copy-start.14
  881.2 14.8 slice-start.3
  881.2 14.8 slice-start.4
  896.0 9.5 copy-start.54
  917.6 256.9 %reduce-scatter.10.cloned.1.call-start = ((), (), s32[]{:S(2)}) async-start(), calls=%async_computation.19 | async-start | bytes 2621440 | tf_op jit(solution)/shard_map/reduce_scatter | solution.py:211
  1088.8 5.7 copy-start.12
  1088.8 12.0 slice-start
  1094.5 6.3 slice-start.1
  1100.8 3.4 copy-start.20
  1106.7 4.2 copy-start.29
  1113.8 5.0 copy-start.1
  1118.8 4.4 copy-start.30
  1118.8 4.4 copy-start.52
  1123.2 4.2 copy-start.29
  1130.2 3.9 copy-start.26
  1130.2 5.7 copy-start.1
  1135.9 5.1 copy-start.30
  1135.9 5.1 copy-start.52
  1144.0 64.6 %reduce-scatter.12.cloned.1.call-start = ((), (), s32[]{:S(2)}) async-start(), calls=%async_computation.20 | async-start | bytes 2621440 | tf_op jit(solution)/shard_map/reduce_scatter | solution.py:212
  1144.6 110.3 %reduce-scatter.14.cloned.1.call-start = ((), (), s32[]{:S(2)}) async-start(), calls=%async_computation.22 | async-start | bytes 2654208 | tf_op jit(solution)/shard_map/reduce_scatter | solution.py:236
  1149.6 25.0 %copy-start.40 = (f32[512]{0:T(512)S(1)}, f32[512]{0:T(512)}, u32[]{:S(2)}) copy-start(f32[512]{0:T(512)} %copy-done.39) | copy-start | bytes 6148
  1149.6 25.0 %copy-start.50 = (f32[128]{0:T(128)S(1)}, f32[128]{0:T(128)}, u32[]{:S(2)}) copy-start(f32[128]{0:T(128)} %copy-done.49) | copy-start | bytes 1540
  1149.6 151.4 %reduce-scatter.20.cloned.1.call-start = ((), (), s32[]{:S(2)}) async-start(), calls=%async_computation.25 | async-start | bytes 2654208 | tf_op jit(solution)/shard_map/reduce_scatter | solution.py:245
  1154.5 186.4 %reduce-scatter.16.cloned.1.call-start = ((), (), s32[]{:S(2)}) async-start(), calls=%async_computation.23 | async-start | bytes 1327104 | tf_op jit(solution)/shard_map/reduce_scatter | solution.py:239
  1179.0 202.1 %reduce-scatter.18.cloned.1.call-start = ((), (), s32[]{:S(2)}) async-start(), calls=%async_computation.24 | async-start | bytes 1327104 | tf_op jit(solution)/shard_map/reduce_scatter | solution.py:242
  1211.7 268.0 %all-reduce.18.cloned.1.call-start = ((), (), s32[]{:S(2)}) async-start(), calls=%async_computation.21 | async-start | bytes 4718592 | tf_op jit(solution)/shard_map/psum | solution.py:225
  1217.8 346.6 %reduce-scatter.26.cloned.1.call-start = ((), (), s32[]{:S(2)}) async-start(), calls=%async_computation.28 | async-start | bytes 11943936 | tf_op jit(solution)/shard_map/reduce_scatter | solution.py:260
  1228.4 421.8 %reduce-scatter.22.cloned.1.call-start = ((), (), s32[]{:S(2)}) async-start(), calls=%async_computation.26 | async-start | bytes 11943936 | tf_op jit(solution)/shard_map/reduce_scatter | solution.py:254
  1238.7 497.1 %reduce-scatter.24.cloned.1.call-start = ((), (), s32[]{:S(2)}) async-start(), calls=%async_computation.27 | async-start | bytes 11943936 | tf_op jit(solution)/shard_map/reduce_scatter | solution.py:257
  1249.5 233.7 %copy-start.43 = (bf16[2304]{0:T(1024)(128)(2,1)S(1)}, bf16[2304]{0:T(1024)(128)(2,1)}, u32[]{:S(2)}) copy-start(bf16[2304]{0:T(1024)(128)(2,1)} %get-tuple-element.654) | copy-start | bytes 13828
  1249.5 233.7 %copy-start.44 = (bf16[2304]{0:T(1024)(128)(2,1)S(1)}, bf16[2304]{0:T(1024)(128)(2,1)}, u32[]{:S(2)}) copy-start(bf16[2304]{0:T(1024)(128)(2,1)} %get-tuple-element.656) | copy-start | bytes 13828
  1249.5 233.7 %copy-start.45 = (bf16[2304]{0:T(1024)(128)(2,1)S(1)}, bf16[2304]{0:T(1024)(128)(2,1)}, u32[]{:S(2)}) copy-start(bf16[2304]{0:T(1024)(128)(2,1)} %get-tuple-element.652) | copy-start | bytes 13828
  (28 other events, 60.9 us)
Sparse Core Ops, SparseCore 0:
  9.9 26.9 all-gather.14
  38.7 24.1 all-gather.16
  65.0 16.7 all-gather.28
  83.6 28.9 all-gather.12
  114.6 16.7 all-gather.18
  133.1 29.0 all-gather.20
  167.7 322.5 all-gather.30
  492.3 62.6 all-gather.22
  556.8 63.8 all-gather.24
  622.4 63.8 all-gather.26
  698.1 171.9 all-reduce.13
  917.8 170.9 all-reduce.15
  1144.1 30.4 reduce-scatter.9
  1177.1 31.4 reduce-scatter.11
  1212.4 42.5 reduce-scatter.13
  1258.5 42.4 reduce-scatter.19
  1304.0 36.7 reduce-scatter.15
  1344.3 36.7 reduce-scatter.17
  1384.1 95.6 all-reduce.17
  1483.1 81.2 reduce-scatter.25
  1567.9 82.2 reduce-scatter.21
  1653.6 82.1 reduce-scatter.23
